TPU v7x, 32 devices: a whole 2x2x4 slice. The times are simulated.
32 devices in a mesh: ctx: 8 (over z, x), tp: 4 (over y, core).
Axes of the slice: x: 2, y: 2, z: 4, core: 2. Of those that a mesh axis runs over, the one named last changes fastest.
Arguments:
- projected: bfloat16 [1024, 3, 4096], P('ctx', None, 'tp'), may hold values from -6 to 6
- short_filter: float32 [7, 3, 4096], P(None, None, 'tp'), may hold values from -2.4 to 2.4
- long_filter: bfloat16 [256, 512], P('tp'), may hold values from -0.53033009 to 0.53033009
- out_weight: bfloat16 [4096, 8192], P('tp'), may hold values from -0.09375 to 0.09375
Outputs:
- layer_out: bfloat16 [1024, 8192], P('ctx', 'tp')
All inputs are finite; a program needn't handle non-finite values.
Results may differ from a plain program's by a relative error of at most 0.015.
Values may be sent and summed in bfloat16 or wider, within the bound.
A program may use at most 64 MiB of HBM per device.

v0:
```python
import jax
import jax.numpy as jnp
from jax import lax
from jax.sharding import PartitionSpec as P

GSIZE = 16


def shifted(array, axis, by):
    size = lax.axis_size(axis)
    pairs = [(i, i + by) for i in range(size) if 0 <= i + by < size]
    return lax.ppermute(array, axis, pairs)


def toeplitz_block(padded_taps, lag_base, count, tok_rows):
    width = tok_rows + count - 1
    groups = padded_taps.shape[0]
    window = lax.dynamic_slice_in_dim(padded_taps, lag_base - (count - 1) + 2 * tok_rows, width, 1)
    flipped = jnp.concatenate([window[:, ::-1], jnp.zeros((groups, 1), window.dtype)], axis=1)
    tiled = jnp.tile(flipped, (1, tok_rows))
    skewed = tiled[:, : tok_rows * width].reshape(groups, tok_rows, width)
    return skewed[:, :, tok_rows - 1 : tok_rows - 1 + count]


def body(projected, short_filter, long_filter, out_weight):
    tok_rows = projected.shape[0]
    taps = short_filter.shape[0]
    groups = long_filter.shape[0]
    reach = long_filter.shape[1]
    border = shifted(projected[tok_rows - (taps - 1) :], "ctx", 1)
    extended = jnp.concatenate([border, projected], axis=0).astype(jnp.float32)
    conved = short_filter[0] * extended[taps - 1 : taps - 1 + tok_rows]
    for offset in range(1, taps):
        conved = (
            conved
            + short_filter[offset] * extended[taps - 1 - offset : taps - 1 - offset + tok_rows]
        )
    values = (conved[:, 1, :] * conved[:, 2, :]).astype(jnp.bfloat16)
    padding = jnp.zeros((groups, 2 * tok_rows), long_filter.dtype)
    padded_taps = jnp.concatenate([padding, long_filter, padding], axis=1)
    lanes = lax.axis_size("ctx")
    whole = lax.all_to_all(values, "ctx", split_axis=1, concat_axis=0, tiled=True)
    share = whole.shape[1]
    held_groups = max(1, share // GSIZE)
    per_group = share // held_groups
    first_group = lax.axis_index("ctx") * share // GSIZE
    own_taps = lax.dynamic_slice_in_dim(padded_taps, first_group, held_groups, 0)
    behind = reach // tok_rows
    lead = jnp.zeros((behind * tok_rows, share), whole.dtype)
    stretched = jnp.concatenate([lead, whole], axis=0)
    blocks = stretched.reshape(behind + lanes, tok_rows, held_groups, per_group)

    def one_lag(step, total):
        matrix = toeplitz_block(own_taps, step * tok_rows, tok_rows, tok_rows)
        source = lax.dynamic_slice_in_dim(blocks, behind - step, lanes, 0)
        return total + jnp.einsum(
            "gts,osgi->otgi", matrix, source, preferred_element_type=jnp.float32
        )

    start_total = jnp.zeros((lanes, tok_rows, held_groups, per_group), jnp.float32)
    spread = lax.fori_loop(0, behind + 1, one_lag, start_total).reshape(lanes * tok_rows, share)
    mixed = lax.all_to_all(
        spread.astype(jnp.bfloat16), "ctx", split_axis=0, concat_axis=1, tiled=True
    ).astype(spread.dtype)
    hidden = (conved[:, 0, :] * mixed).astype(jnp.bfloat16)
    partial_sum = jnp.dot(hidden, out_weight, preferred_element_type=jnp.float32)
    return lax.psum_scatter(partial_sum.astype(jnp.bfloat16), "tp", scatter_dimension=1, tiled=True)


def solution(mesh):
    return jax.shard_map(
        body,
        mesh=mesh,
        in_specs=(P("ctx", None, "tp"), P(None, None, "tp"), P("tp", None), P("tp", None)),
        out_specs=P("ctx", "tp"),
        check_vma=False,
    )
```

profile of v0, /device:TPU:0, one launch (start us, length us, event | category | flops | bytes accessed | tf_op | source)
XLA Modules:
  0.0 110.3 jit_solution(17696576427877202739)
XLA Ops:
  6.5 0.8 slice.81
  7.3 4.8 %collective-permute-start = (bf16[6,3,1024]{2,0,1:T(8,128)(2,1)S(1)}, bf16[6,3,1024]{2,0,1:T(8,128)(2,1)S(1)}, u32[]{:S(2)}, u32[]{:S(2)}) collective-permute-start(bf16[6,3,1024]{2,0,1:T(8,128)(2,1)S(1)} %slice.81), channel_id=1, source_target_pairs={{0,4},{4,8},{8,12},{12,16},{16,20},{20,24},{24,28},{1,5},{5,9},{9,... | collective-permute-start | bytes 110600 | tf_op jit(solution)/shard_map/ppermute | solution.py:12
  12.2 1.5 %fusion.13 = (f32[1,3,1024]{2,0,1:T(1,128)S(1)}, f32[1,3,1024]{2,0,1:T(1,128)S(1)}, f32[1,3,1024]{2,0,1:T(1,128)S(1)}, f32[1,3,1024]{2,0,1:T(1,128)S(1)}, f32[1,...) fusion(f32[7,3,1024]{2,0,1:T(8,128)} %param.7), kind=kLoop, calls=%fused_computation.39 | loop fusion | bytes 172032 | tf_op jit(solution)/shard_map/slice | solution.py:32
  13.8 1.5 %copy.16 = bf16[128,3,1024]{0,2,1:T(8,128)(2,1)S(1)} copy(bf16[128,3,1024]{2,0,1:T(8,128)(2,1)} %param.6) | data formatting | bytes 1572864 | tf_op args[0]
  15.3 0.4 copy.15
  15.7 0.6 maximum_convert_fusion
  16.3 5.9 %fusion.2 = f32[128,3,1024]{0,2,1:T(8,128)S(1)} fusion(f32[134,3,1024]{0,2,1:T(8,128)S(1)} %maximum_convert_fusion, f32[3,1024]{1,0:T(4,128)S(1)} %get-tuple-element.192, f32[3,1024]{1,0:T(4,128)S(1)} %get-tuple-element.193, f32[3,1024]{1,0:T(4,128)S(1)} %get-tuple-element.194, f32[3,1024]{1,0:T(4,128)S(1)} %get-tuple-element.195, ...), kind=kLoop, calls=%fused_computation.8 | loop fusion | flops 5111808 | bytes 12668928 | tf_op jit(solution)/shard_map/add | solution.py:35
  22.2 1.1 %copy-done = f32[128,3,1024]{0,2,1:T(8,128)} copy-done((f32[128,3,1024]{0,2,1:T(8,128)}, f32[128,3,1024]{0,2,1:T(8,128)S(1)}, u32[]{:S(2)}) %copy-start) | copy-done | bytes 1572888
  23.4 0.8 fusion.8
  24.1 5.3 %all-to-all-start = ((bf16[128,8,128]{0,2,1:T(8,128)(2,1)}), bf16[128,8,128]{0,2,1:T(8,128)(2,1)S(1)}, u32[]{:S(2)}, u32[]{:S(2)}) async-start(bf16[128,8,128]{0,2,1:T(8,128)(2,1)} %bitcast.1), calls=%async_computation | async-start | bytes 524288 | tf_op jit(solution)/shard_map/all_to_all | solution.py:42
  29.6 8.2 %all-to-all-done = bf16[128,8,128]{0,2,1:T(8,128)(2,1)S(1)} async-done(((bf16[128,8,128]{0,2,1:T(8,128)(2,1)}), bf16[128,8,128]{0,2,1:T(8,128)(2,1)S(1)}, u32[]{:S(2)}, u32[]{:S(2)}) %all-to-all-start) | async-done | bytes 262176 | tf_op jit(solution)/shard_map/all_to_all | solution.py:42
  37.8 0.2 copy.17
  38.2 0.3 reshape.35
  38.5 11.9 %while.18 = (s32[]{:T(128)}, f32[8,128,8,16]{1,3,0,2:T(8,128)S(1)}, bf16[12,128,8,16]{1,0,3,2:T(8,128)(2,1)S(1)}, bf16[8,1024]{1,0:T(8,128)(2,1)S(1)}, s32[]{:T(...) while((s32[]{:T(128)}, f32[8,128,8,16]{1,3,0,2:T(8,128)S(1)}, ...), condition=%wide.region_1.2_spmd.clone, body=%wide.region_0.1_spmd.clone.sunk | while | flops 33816588 | bytes 4747433 | solution.py:61
  38.6 0.2 reverse.2
  38.9 1.4 %reshape.40 = bf16[8,128,255]{2,1,0:T(8,128)(2,1)S(1)} reshape(bf16[8,32640]{1,0:T(8,128)(2,1)S(1)} %slice.167) | data formatting | bytes 1044480 | tf_op jit(solution)/shard_map/while/body/eval_jaxpr/reshape | solution.py:21
  40.4 0.4 fusion.19
  41.0 0.2 reverse.2
  41.3 1.4 %reshape.40 = bf16[8,128,255]{2,1,0:T(8,128)(2,1)S(1)} reshape(bf16[8,32640]{1,0:T(8,128)(2,1)S(1)} %slice.167) | data formatting | bytes 1044480 | tf_op jit(solution)/shard_map/while/body/eval_jaxpr/reshape | solution.py:21
  42.8 0.4 fusion.19
  43.3 0.2 reverse.2
  43.7 1.4 %reshape.40 = bf16[8,128,255]{2,1,0:T(8,128)(2,1)S(1)} reshape(bf16[8,32640]{1,0:T(8,128)(2,1)S(1)} %slice.167) | data formatting | bytes 1044480 | tf_op jit(solution)/shard_map/while/body/eval_jaxpr/reshape | solution.py:21
  45.2 0.4 fusion.19
  45.7 0.2 reverse.2
  46.1 1.4 %reshape.40 = bf16[8,128,255]{2,1,0:T(8,128)(2,1)S(1)} reshape(bf16[8,32640]{1,0:T(8,128)(2,1)S(1)} %slice.167) | data formatting | bytes 1044480 | tf_op jit(solution)/shard_map/while/body/eval_jaxpr/reshape | solution.py:21
  47.6 0.4 fusion.19
  48.5 1.4 %reshape.40 = bf16[8,128,255]{2,1,0:T(8,128)(2,1)S(1)} reshape(bf16[8,32640]{1,0:T(8,128)(2,1)S(1)} %slice.167) | data formatting | bytes 1044480 | tf_op jit(solution)/shard_map/while/body/eval_jaxpr/reshape | solution.py:21
  50.0 0.4 fusion.19
  50.5 11.8 %all_to_all.26 = bf16[8,128,128]{1,2,0:T(8,128)(2,1)S(1)} all-to-all(bf16[8,128,128]{1,2,0:T(8,128)(2,1)S(1)} %bitcast.53), channel_id=1, replica_groups=mesh['ctx'=8,'tp'=4] {'ctx'}, dimensions={0} | all-to-all | bytes 524288 | tf_op jit(solution)/shard_map/all_to_all | solution.py:62
  62.2 1.1 fusion.10
  63.3 9.6 %convolution_convert_fusion = bf16[128,8192]{1,0:T(8,128)(2,1)} fusion(bf16[128,1024]{0,1:T(8,128)(2,1)S(1)} %fusion.10, bf16[1024,8192]{1,0:T(8,128)(2,1)} %param.9), kind=kOutput, calls=%fused_computation.6 | convolution fusion | flops 2148532224 | bytes 19136512 | tf_op jit(solution)/shard_map/dot_general | solution.py:66
  72.9 30.5 %reduce-scatter.2.cloned.1.call-done = bf16[128,2048]{1,0:T(8,128)(2,1)} async-done(((bf16[128,8192]{1,0:T(8,128)(2,1)}), bf16[128,2048]{1,0:T(8,128)(2,1)}) %reduce-scatter.2.cloned.1.call-update) | async-done | bytes 524304 | tf_op jit(solution)/shard_map/reduce_scatter | solution.py:67
  (47 shorter events, 2.3 us)
Async XLA Ops:
  7.3 7.9 %collective-permute-start = (bf16[6,3,1024]{2,0,1:T(8,128)(2,1)S(1)}, bf16[6,3,1024]{2,0,1:T(8,128)(2,1)S(1)}, u32[]{:S(2)}, u32[]{:S(2)}) collective-permute-start(bf16[6,3,1024]{2,0,1:T(8,128)(2,1)S(1)} %slice.81), channel_id=1, source_target_pairs={{0,4},{4,8},{8,12},{12,16},{16,20},{20,24},{24,28},{1,5},{5,9},{9,... | collective-permute-start | bytes 110600 | tf_op jit(solution)/shard_map/ppermute | solution.py:12
  22.2 1.2 %copy-start = (f32[128,3,1024]{0,2,1:T(8,128)}, f32[128,3,1024]{0,2,1:T(8,128)S(1)}, u32[]{:S(2)}) copy-start(f32[128,3,1024]{0,2,1:T(8,128)S(1)} %fusion.2) | copy-start | bytes 4718596
  23.4 6.1 %copy-start.1 = (bf16[64,512]{1,0:T(8,128)(2,1)S(1)}, bf16[64,512]{1,0:T(8,128)(2,1)}, u32[]{:S(2)}) copy-start(bf16[64,512]{1,0:T(8,128)(2,1)} %param.8) | copy-start | bytes 196612
  24.1 13.7 %all-to-all-start = ((bf16[128,8,128]{0,2,1:T(8,128)(2,1)}), bf16[128,8,128]{0,2,1:T(8,128)(2,1)S(1)}, u32[]{:S(2)}, u32[]{:S(2)}) async-start(bf16[128,8,128]{0,2,1:T(8,128)(2,1)} %bitcast.1), calls=%async_computation | async-start | bytes 524288 | tf_op jit(solution)/shard_map/all_to_all | solution.py:42
  29.4 74.0 %reduce-scatter.2.cloned.1.call-start = ((), (), s32[]{:S(2)}) async-start(), calls=%async_computation.3 | async-start | bytes 2621440 | tf_op jit(solution)/shard_map/reduce_scatter | solution.py:67
Sparse Core Ops, SparseCore 0:
  73.0 30.3 reduce-scatter.1
where the time goes:
time: 111 us; the launch traced here: 110 us
  waiting for transfers between devices  38.8 us (35%)
  local copies, waits for them, and re-layouts  15.5 us (14%)
  between operations  13.6 us (12%)
  matrix products  11.8 us (11%)
  blocking collectives  11.8 us (11%)
  starting transfers between devices  10.2 us (9%)
  other arithmetic  8.39 us (8%)
    reduce_scatter x1, waiting for transfers between devices, body(): lax.psum_scatter(partial_sum.astype(jnp.bfloat16), 'tp', scatter_dimensio...  30.5 us
    all_to_all x1, blocking collectives, body(): lax.all_to_all(spread.astype(jnp.bfloat16), 'ctx', split_axis=0, concat_a...  11.8 us
    dot_general x1, matrix products, body(): jnp.dot(hidden, out_weight, preferred_element_type=jnp.float32)  9.58 us
    all_to_all x1, waiting for transfers between devices, body(): lax.all_to_all(values, 'ctx', split_axis=1, concat_axis=0, tiled=True)  8.23 us
    reshape x5, local copies, waits for them, and re-layouts, toeplitz_block(): skewed = tiled[:, :tok_rows * width].reshape(groups, tok_rows, width)  6.82 us
    add x1, other arithmetic, body(): conved + short_filter[offset] * extended[taps - 1 - offset:taps - 1 - off...  5.88 us
    all_to_all x1, starting transfers between devices, body(): lax.all_to_all(values, 'ctx', split_axis=1, concat_axis=0, tiled=True)  5.28 us
    ppermute x1, starting transfers between devices, shifted(): return lax.ppermute(array, axis, pairs)  4.84 us
  transfers between devices with their start and end apart: 3, of which 2 were waited for; matrix products, arithmetic and copies ran while one was open for 3% of the time, Pallas kernels for 0%

commit v1 on v0

--- a/solution.py
+++ b/solution.py
@@ -1,9 +1,324 @@
+import functools
+
 import jax
 import jax.numpy as jnp
 from jax import lax
+from jax.experimental import pallas as pl
+from jax.experimental.pallas import tpu as pltpu
 from jax.sharding import PartitionSpec as P
 
 GSIZE = 16
+EDGE = 16
+
+
+def aligned(start, size):
+    return pl.ds(pl.multiple_of(start, size), size)
+
+
+def fused_kernel(
+    lanes,
+    cores_y,
+    proj,
+    short,
+    longf,
+    weight,
+    out,
+    held_weight,
+    border,
+    padded,
+    toeplitz,
+    gate,
+    send_v,
+    recv_v,
+    send_m,
+    recv_m,
+    hidden,
+    core_send,
+    core_recv,
+    y_send,
+    y_recv,
+    w_sem,
+    edge_sem,
+    v_sems,
+    v_recvs,
+    m_sems,
+    m_recvs,
+    cs_sems,
+    cr_sems,
+    ys_sems,
+    yr_sems,
+):
+    me = lax.axis_index("ctx")
+    tp = lax.axis_index("tp")
+    y, core = tp // 2, tp % 2
+    partner = y * 2 + (1 - core)
+    _, rows, chans = proj.shape
+    taps = short.shape[0]
+    reach = longf.shape[1]
+    behind = reach // rows
+    share = chans // lanes
+    own_groups = share // GSIZE
+    pieces, wide = y_send.shape[1], y_send.shape[3]
+
+    load = pltpu.make_async_copy(weight, held_weight, w_sem)
+    load.start()
+
+    barrier = pltpu.get_barrier_semaphore()
+    for k in range(1, lanes):
+        pl.semaphore_signal(barrier, inc=1, device_id={"ctx": lax.rem(me + k, lanes)})
+    pl.semaphore_signal(barrier, inc=1, device_id={"tp": partner})
+    for dy in range(1, cores_y):
+        pl.semaphore_signal(
+            barrier, inc=1, device_id={"tp": lax.rem(y + dy, cores_y) * 2 + core}
+        )
+    pl.semaphore_wait(barrier, lanes - 1 + 1 + cores_y - 1)
+
+    edge = pltpu.make_async_remote_copy(
+        src_ref=proj.at[:, pl.ds(rows - EDGE, EDGE), :],
+        dst_ref=border,
+        send_sem=edge_sem.at[0],
+        recv_sem=edge_sem.at[1],
+        device_id={"ctx": lax.rem(me + 1, lanes)},
+    )
+    edge.start()
+
+    groups = longf.shape[0]
+    padded[:, 0:rows] = jnp.zeros((groups, rows), jnp.float32)
+    padded[:, rows : rows + reach] = longf[...].astype(jnp.float32)
+    padded[:, rows + reach :] = jnp.zeros((groups, rows), jnp.float32)
+    recv_v[0:behind] = jnp.zeros((behind, share, rows), jnp.bfloat16)
+
+    def build(g, _):
+        line = padded[pl.ds(me * own_groups + g, 1), :]
+        flat = jnp.broadcast_to(line, (rows, reach + 2 * rows))
+        skewed = pltpu.roll(flat, 0, 1, stride=1, stride_axis=0)
+        for b in range(behind + 1):
+            low = rows + reach - rows * b
+            toeplitz[g, b * rows : (b + 1) * rows, :] = skewed[:, low : low + rows].astype(jnp.bfloat16)
+        return 0
+
+    lax.fori_loop(0, own_groups, build, 0)
+    edge.wait()
+
+    def conv(p, j):
+        cols = aligned(j * share, share)
+        before = jnp.where(me == 0, 0.0, border[p, :, cols].astype(jnp.float32))
+        ext = jnp.concatenate([before, proj[p, :, cols].astype(jnp.float32)], axis=0)
+        total = short[0, p : p + 1, cols] * ext[EDGE:]
+        for d in range(1, taps):
+            total = total + short[d, p : p + 1, cols] * pltpu.roll(ext, d, 0)[EDGE:]
+        return total
+
+    def values_of(j):
+        return (conv(1, j) * conv(2, j)).T.astype(jnp.bfloat16)
+
+    def values_copy(slot, peer):
+        return pltpu.make_async_remote_copy(
+            src_ref=send_v.at[peer],
+            dst_ref=recv_v.at[behind + slot],
+            send_sem=v_sems.at[peer],
+            recv_sem=v_recvs.at[slot],
+            device_id={"ctx": peer},
+        )
+
+    def mixed_copy(slot, peer):
+        return pltpu.make_async_remote_copy(
+            src_ref=send_m.at[peer],
+            dst_ref=recv_m.at[slot],
+            send_sem=m_sems.at[peer],
+            recv_sem=m_recvs.at[slot],
+            device_id={"ctx": peer},
+        )
+
+    def send_values(k, _):
+        peer = lax.rem(me + k, lanes)
+        send_v[peer] = values_of(peer)
+        values_copy(me, peer).start()
+        return 0
+
+    lax.fori_loop(1, lanes, send_values, 0)
+    recv_v[behind + me] = values_of(me)
+
+    def gates(j, _):
+        gate[:, aligned(j * share, share)] = conv(0, j)
+        return 0
+
+    lax.fori_loop(0, lanes, gates, 0)
+
+    def take_values(k, _):
+        peer = lax.rem(me + k, lanes)
+        values_copy(peer, peer).wait_recv()
+        return 0
+
+    lax.fori_loop(1, lanes, take_values, 0)
+
+    for g in range(own_groups):
+        part = pl.ds(g * GSIZE, GSIZE)
+        lhs = jnp.concatenate(
+            [recv_v[b : b + lanes, part, :].reshape(lanes * GSIZE, rows) for b in range(behind + 1)],
+            axis=1,
+        )
+        mixed = jnp.dot(lhs, toeplitz[g], preferred_element_type=jnp.float32)
+        send_m[:, part, :] = mixed.astype(jnp.bfloat16).reshape(lanes, GSIZE, rows)
+
+    def send_mixed(k, _):
+        mixed_copy(me, lax.rem(me + k, lanes)).start()
+        return 0
+
+    lax.fori_loop(1, lanes, send_mixed, 0)
+    recv_m[me] = send_m[me]
+
+    def make_hidden(j):
+        cols = aligned(j * share, share)
+        mixed = recv_m[j].astype(jnp.float32).T
+        hidden[:, cols] = (gate[:, cols] * mixed).astype(jnp.bfloat16)
+
+    make_hidden(me)
+
+    def take_mixed(k, _):
+        peer = lax.rem(me + k, lanes)
+        mixed_copy(peer, peer).wait_recv()
+        make_hidden(peer)
+        return 0
+
+    lax.fori_loop(1, lanes, take_mixed, 0)
+    load.wait()
+
+    def product(device, q):
+        cols = aligned((device * pieces + q) * wide, wide)
+        return jnp.dot(hidden[...], held_weight[:, cols], preferred_element_type=jnp.float32)
+
+    def core_copy(dy, q):
+        return pltpu.make_async_remote_copy(
+            src_ref=core_send.at[dy, q],
+            dst_ref=core_recv.at[dy, q],
+            send_sem=cs_sems.at[dy, q],
+            recv_sem=cr_sems.at[dy, q],
+            device_id={"tp": partner},
+        )
+
+    def y_copy(dy, q):
+        return pltpu.make_async_remote_copy(
+            src_ref=y_send.at[dy, q],
+            dst_ref=y_recv.at[dy, q],
+            send_sem=ys_sems.at[dy, q],
+            recv_sem=yr_sems.at[dy, q],
+            device_id={"tp": lax.rem(y + dy, cores_y) * 2 + core},
+        )
+
+    for dy in list(range(1, cores_y)) + [0]:
+        other = lax.rem(y + dy, cores_y) * 2
+
+        def give(q, _):
+            core_send[dy, q] = product(other + 1 - core, q).astype(jnp.bfloat16)
+            core_copy(dy, q).start()
+            return 0
+
+        lax.fori_loop(0, pieces, give, 0)
+
+        def add(q, _):
+            mine = product(other + core, q)
+            core_copy(dy, q).wait_recv()
+            mine = mine + core_recv[dy, q].astype(jnp.float32)
+            if dy:
+                y_send[dy, q] = mine.astype(jnp.bfloat16)
+                y_copy(dy, q).start()
+            else:
+                for other_dy in range(1, cores_y):
+                    y_copy(other_dy, q).wait_recv()
+                    mine = mine + y_recv[other_dy, q].astype(jnp.float32)
+                out[:, aligned(q * wide, wide)] = mine.astype(jnp.bfloat16)
+            return 0
+
+        lax.fori_loop(0, pieces, add, 0)
+
+    def drain(k, _):
+        peer = lax.rem(me + k, lanes)
+        values_copy(me, peer).wait_send()
+        mixed_copy(me, peer).wait_send()
+        return 0
+
+    lax.fori_loop(1, lanes, drain, 0)
+    for dy in range(cores_y):
+
+        def drain_sum(q, _):
+            core_copy(dy, q).wait_send()
+            if dy:
+                y_copy(dy, q).wait_send()
+            return 0
+
+        lax.fori_loop(0, pieces, drain_sum, 0)
+
+
+def fused(projected, short_filter, long_filter, out_weight):
+    lanes, devices = lax.axis_size("ctx"), lax.axis_size("tp")
+    rows, _, chans = projected.shape
+    groups, reach = long_filter.shape
+    features = out_weight.shape[1]
+    cores_y = devices // 2
+    share = chans // lanes
+    behind = reach // rows
+    own = features // devices
+    pieces = 4
+    wide = own // pieces
+    bf16, f32 = jnp.bfloat16, jnp.float32
+    vmem = pl.BlockSpec(memory_space=pltpu.VMEM)
+    dma = pltpu.SemaphoreType.DMA
+    return pl.pallas_call(
+        functools.partial(fused_kernel, lanes, cores_y),
+        out_shape=jax.ShapeDtypeStruct((rows, own), bf16),
+        in_specs=[vmem, vmem, vmem, pl.BlockSpec(memory_space=pl.ANY)],
+        out_specs=vmem,
+        scratch_shapes=[
+            pltpu.VMEM((chans, features), bf16),
+            pltpu.VMEM((3, EDGE, chans), bf16),
+            pltpu.VMEM((groups, reach + 2 * rows), f32),
+            pltpu.VMEM((share // GSIZE, reach + rows, rows), bf16),
+            pltpu.VMEM((rows, chans), f32),
+            pltpu.VMEM((lanes, share, rows), bf16),
+            pltpu.VMEM((behind + lanes, share, rows), bf16),
+            pltpu.VMEM((lanes, share, rows), bf16),
+            pltpu.VMEM((lanes, share, rows), bf16),
+            pltpu.VMEM((rows, chans), bf16),
+            pltpu.VMEM((cores_y, pieces, rows, wide), bf16),
+            pltpu.VMEM((cores_y, pieces, rows, wide), bf16),
+            pltpu.VMEM((cores_y, pieces, rows, wide), bf16),
+            pltpu.VMEM((cores_y, pieces, rows, wide), bf16),
+            dma,
+            dma((2,)),
+            dma((lanes,)),
+            dma((lanes,)),
+            dma((lanes,)),
+            dma((lanes,)),
+            dma((cores_y, pieces)),
+            dma((cores_y, pieces)),
+            dma((cores_y, pieces)),
+            dma((cores_y, pieces)),
+        ],
+        compiler_params=pltpu.CompilerParams(
+            collective_id=0, has_side_effects=True, vmem_limit_bytes=48 * 2**20
+        ),
+        cost_estimate=pl.CostEstimate(
+            flops=2 * rows * chans * features,
+            bytes_accessed=2 * chans * features,
+            transcendentals=0,
+        ),
+    )(jnp.transpose(projected, (1, 0, 2)), short_filter, long_filter, out_weight)
+
+
+def fits(projected, long_filter, out_weight):
+    lanes, devices = lax.axis_size("ctx"), lax.axis_size("tp")
+    rows, _, chans = projected.shape
+    share = chans // lanes
+    return (
+        rows % 128 == 0
+        and share % 128 == 0
+        and share * lanes == chans
+        and lanes > 1
+        and devices % 2 == 0
+        and long_filter.shape[1] % rows == 0
+        and out_weight.shape[1] % (devices * 512) == 0
+    )
 
 
 def shifted(array, axis, by):
@@ -23,6 +338,8 @@
 
 
 def body(projected, short_filter, long_filter, out_weight):
+    if fits(projected, long_filter, out_weight):
+        return fused(projected, short_filter, long_filter, out_weight)
     tok_rows = projected.shape[0]
     taps = short_filter.shape[0]
     groups = long_filter.shape[0]

time: 111 us -> 44.1 us (0.40)
  Pallas kernels: 0 us -> 40.1 us
  waiting for transfers between devices: 38.8 us -> 0 us
  between operations: 13.6 us -> 0.02 us
  matrix products: 11.8 us -> 0 us
  blocking collectives: 11.8 us -> 0 us
  local copies, waits for them, and re-layouts: 15.5 us -> 3.72 us
  starting transfers between devices: 10.2 us -> 0 us
  other arithmetic: 8.39 us -> 0 us
    pallas_call x0 -> x1, Pallas kernels: none -> 40.1 us  [fused(): pl.pallas_call(functools.partial(fused_kernel, lanes, cores_y), out_shape...]
    reduce_scatter x1 -> x0, waiting for transfers between devices: 30.5 us -> none  [body(): lax.psum_scatter(partial_sum.astype(jnp.bfloat16), 'tp', scatter_dimensio...]
    dot_general x6 -> x0, matrix products: 11.8 us -> none  [the longest x1 9.58 us: body(): jnp.dot(hidden, out_weight, preferred_element_type=jnp.float32)]
    all_to_all x1 -> x0, blocking collectives: 11.8 us -> none  [body(): lax.all_to_all(spread.astype(jnp.bfloat16), 'ctx', split_axis=0, concat_a...]
    all_to_all x1 -> x0, waiting for transfers between devices: 8.23 us -> none  [body(): lax.all_to_all(values, 'ctx', split_axis=1, concat_axis=0, tiled=True)]
    reshape x6 -> x0, local copies, waits for them, and re-layouts: 7.1 us -> none  [the longest x5 6.82 us: toeplitz_block(): skewed = tiled[:, :tok_rows * width].reshape(groups, tok_rows, width)]
    add x1 -> x0, other arithmetic: 5.88 us -> none  [body(): conved + short_filter[offset] * extended[taps - 1 - offset:taps - 1 - off...]
    all_to_all x1 -> x0, starting transfers between devices: 5.28 us -> none  [body(): lax.all_to_all(values, 'ctx', split_axis=1, concat_axis=0, tiled=True)]
  transfers between devices with their start and end apart: 3 -> 0, of which waited for: 2 -> 0; matrix products, arithmetic and copies ran while one was open for 3% -> 0% of each run, Pallas kernels for 0% -> 0%
where the time goes in v1:
time: 44.1 us; the launch traced here: 43.8 us
  Pallas kernels  40.1 us (91%)
  local copies, waits for them, and re-layouts  3.72 us (8%)
    pallas_call x1, Pallas kernels, fused(): pl.pallas_call(functools.partial(fused_kernel, lanes, cores_y), out_shape...  40.1 us
    unnamed x6, local copies, waits for them, and re-layouts  3.72 us

profile of v1, /device:TPU:0, one launch (start us, length us, event | category | flops | bytes accessed | tf_op | source)
XLA Modules:
  0.0 43.8 jit_solution(10130331994285880014)
XLA Ops:
  0.0 1.0 %copy.5.short = f32[7,3,1024]{2,1,0:T(4,128)S(1)} copy(f32[7,3,1024]{2,0,1:T(8,128)} %param.5) | data formatting | bytes 172032 | tf_op args[1]
  1.0 0.0 copy-start
  1.0 1.1 %copy-done = bf16[128,3,1024]{2,0,1:T(8,128)(2,1)S(1)} copy-done((bf16[128,3,1024]{2,0,1:T(8,128)(2,1)S(1)}, bf16[128,3,1024]{2,0,1:T(8,128)(2,1)}, u32[]{:S(2)}) %copy-start) | copy-done | bytes 786456
  2.1 0.0 copy-start.1
  2.1 0.8 %copy-done.1 = bf16[64,512]{1,0:T(8,128)(2,1)S(1)} copy-done((bf16[64,512]{1,0:T(8,128)(2,1)S(1)}, bf16[64,512]{1,0:T(8,128)(2,1)}, u32[]{:S(2)}) %copy-start.1) | copy-done | bytes 65560
  2.9 40.1 %shard_map.46 = bf16[128,2048]{1,0:T(8,128)(2,1)S(1)} custom-call(bf16[3,128,1024]{2,1,0:T(8,128)(2,1)S(1)} %bitcast.1, f32[7,3,1024]{2,1,0:T(4,128)S(1)} %copy.5.short, bf16[64,512]{1,0:T(8,128)(2,1)S(1)} %copy-done.1, bf16[1024,8192]{1,0:T(8,128)(2,1)} %weight.1), custom_call_target="tpu_custom_call" | custom-call | flops 2147483648 | bytes 16777216 | tf_op jit(solution)/shard_map/pallas_call | solution.py:267
  43.0 0.8 %copy.7 = bf16[128,2048]{1,0:T(8,128)(2,1)} copy(bf16[128,2048]{1,0:T(8,128)(2,1)S(1)} %shard_map.46) | data formatting | bytes 1048576
Async XLA Ops:
  1.0 1.1 %copy-start = (bf16[128,3,1024]{2,0,1:T(8,128)(2,1)S(1)}, bf16[128,3,1024]{2,0,1:T(8,128)(2,1)}, u32[]{:S(2)}) copy-start(bf16[128,3,1024]{2,0,1:T(8,128)(2,1)} %param.4) | copy-start | bytes 2359300
  2.1 0.8 %copy-start.1 = (bf16[64,512]{1,0:T(8,128)(2,1)S(1)}, bf16[64,512]{1,0:T(8,128)(2,1)}, u32[]{:S(2)}) copy-start(bf16[64,512]{1,0:T(8,128)(2,1)} %longf.1) | copy-start | bytes 196612

commit v2 on v1

--- a/solution.py
+++ b/solution.py
@@ -18,16 +18,20 @@
 def fused_kernel(
     lanes,
     cores_y,
+    proj_hbm,
+    short_hbm,
+    longf_hbm,
+    weight,
+    out,
     proj,
     short,
     longf,
-    weight,
-    out,
     held_weight,
     border,
     padded,
     toeplitz,
     gate,
+    values,
     send_v,
     recv_v,
     send_m,
@@ -37,7 +41,7 @@
     core_recv,
     y_send,
     y_recv,
-    w_sem,
+    load_sems,
     edge_sem,
     v_sems,
     v_recvs,
@@ -53,15 +57,21 @@
     y, core = tp // 2, tp % 2
     partner = y * 2 + (1 - core)
     _, rows, chans = proj.shape
-    taps = short.shape[0]
+    taps = short.shape[1]
     reach = longf.shape[1]
     behind = reach // rows
     share = chans // lanes
     own_groups = share // GSIZE
     pieces, wide = y_send.shape[1], y_send.shape[3]
 
-    load = pltpu.make_async_copy(weight, held_weight, w_sem)
-    load.start()
+    loads = [
+        pltpu.make_async_copy(source, target, load_sems.at[i])
+        for i, (source, target) in enumerate(
+            [(longf_hbm, longf), (proj_hbm, proj), (short_hbm, short), (weight, held_weight)]
+        )
+    ]
+    for load in loads:
+        load.start()
 
     barrier = pltpu.get_barrier_semaphore()
     for k in range(1, lanes):
@@ -71,17 +81,7 @@
         pl.semaphore_signal(
             barrier, inc=1, device_id={"tp": lax.rem(y + dy, cores_y) * 2 + core}
         )
-    pl.semaphore_wait(barrier, lanes - 1 + 1 + cores_y - 1)
-
-    edge = pltpu.make_async_remote_copy(
-        src_ref=proj.at[:, pl.ds(rows - EDGE, EDGE), :],
-        dst_ref=border,
-        send_sem=edge_sem.at[0],
-        recv_sem=edge_sem.at[1],
-        device_id={"ctx": lax.rem(me + 1, lanes)},
-    )
-    edge.start()
-
+    loads[0].wait()
     groups = longf.shape[0]
     padded[:, 0:rows] = jnp.zeros((groups, rows), jnp.float32)
     padded[:, rows : rows + reach] = longf[...].astype(jnp.float32)
@@ -98,19 +98,49 @@
         return 0
 
     lax.fori_loop(0, own_groups, build, 0)
-    edge.wait()
-
-    def conv(p, j):
+    pl.semaphore_wait(barrier, lanes - 1 + 1 + cores_y - 1)
+
+    edge = pltpu.make_async_remote_copy(
+        src_ref=proj_hbm.at[:, pl.ds(rows - EDGE, EDGE), :],
+        dst_ref=border,
+        send_sem=edge_sem.at[0],
+        recv_sem=edge_sem.at[1],
+        device_id={"ctx": lax.rem(me + 1, lanes)},
+    )
+    edge.start()
+
+
+    loads[1].wait()
+    loads[2].wait()
+
+    def taps_over(ext, p, cols):
+        total = short[p, 0:1, cols] * ext[EDGE:]
+        for d in range(1, taps):
+            total = total + short[p, d : d + 1, cols] * pltpu.roll(ext, d, 0)[EDGE:]
+        return total
+
+    def inner(p, j):
+        return taps_over(proj[p, :, aligned(j * share, share)].astype(jnp.float32), p, aligned(j * share, share))
+
+    def outer(p, j):
         cols = aligned(j * share, share)
         before = jnp.where(me == 0, 0.0, border[p, :, cols].astype(jnp.float32))
-        ext = jnp.concatenate([before, proj[p, :, cols].astype(jnp.float32)], axis=0)
-        total = short[0, p : p + 1, cols] * ext[EDGE:]
-        for d in range(1, taps):
-            total = total + short[d, p : p + 1, cols] * pltpu.roll(ext, d, 0)[EDGE:]
-        return total
+        first = proj[p, 0:EDGE, cols].astype(jnp.float32)
+        return taps_over(jnp.concatenate([before, first], axis=0), p, cols)
+
+    def inner_rows(j, _):
+        cols = aligned(j * share, share)
+        values[EDGE:, cols] = inner(1, j) * inner(2, j)
+        gate[EDGE:, cols] = inner(0, j)
+        return 0
+
+    lax.fori_loop(0, lanes, inner_rows, 0)
+    edge.wait()
 
     def values_of(j):
-        return (conv(1, j) * conv(2, j)).T.astype(jnp.bfloat16)
+        cols = aligned(j * share, share)
+        values[0:EDGE, cols] = outer(1, j) * outer(2, j)
+        return values[:, cols].T.astype(jnp.bfloat16)
 
     def values_copy(slot, peer):
         return pltpu.make_async_remote_copy(
@@ -121,12 +151,15 @@
             device_id={"ctx": peer},
         )
 
-    def mixed_copy(slot, peer):
+    half = share // 2
+
+    def mixed_copy(slot, peer, h):
+        part = pl.ds(h * half, half)
         return pltpu.make_async_remote_copy(
-            src_ref=send_m.at[peer],
-            dst_ref=recv_m.at[slot],
-            send_sem=m_sems.at[peer],
-            recv_sem=m_recvs.at[slot],
+            src_ref=send_m.at[peer, part],
+            dst_ref=recv_m.at[slot, part],
+            send_sem=m_sems.at[h, peer],
+            recv_sem=m_recvs.at[h, slot],
             device_id={"ctx": peer},
         )
 
@@ -140,7 +173,7 @@
     recv_v[behind + me] = values_of(me)
 
     def gates(j, _):
-        gate[:, aligned(j * share, share)] = conv(0, j)
+        gate[0:EDGE, aligned(j * share, share)] = outer(0, j)
         return 0
 
     lax.fori_loop(0, lanes, gates, 0)
@@ -151,6 +184,13 @@
         return 0
 
     lax.fori_loop(1, lanes, take_values, 0)
+
+    def send_mixed(h):
+        def start(k, _):
+            mixed_copy(me, lax.rem(me + k, lanes), h).start()
+            return 0
+
+        lax.fori_loop(1, lanes, start, 0)
 
     for g in range(own_groups):
         part = pl.ds(g * GSIZE, GSIZE)
@@ -160,12 +200,9 @@
         )
         mixed = jnp.dot(lhs, toeplitz[g], preferred_element_type=jnp.float32)
         send_m[:, part, :] = mixed.astype(jnp.bfloat16).reshape(lanes, GSIZE, rows)
-
-    def send_mixed(k, _):
-        mixed_copy(me, lax.rem(me + k, lanes)).start()
-        return 0
-
-    lax.fori_loop(1, lanes, send_mixed, 0)
+        if (g + 1) * GSIZE % half == 0:
+            send_mixed(((g + 1) * GSIZE - 1) // half)
+
     recv_m[me] = send_m[me]
 
     def make_hidden(j):
@@ -177,12 +214,13 @@
 
     def take_mixed(k, _):
         peer = lax.rem(me + k, lanes)
-        mixed_copy(peer, peer).wait_recv()
+        mixed_copy(peer, peer, 0).wait_recv()
+        mixed_copy(peer, peer, 1).wait_recv()
         make_hidden(peer)
         return 0
 
     lax.fori_loop(1, lanes, take_mixed, 0)
-    load.wait()
+    loads[3].wait()
 
     def product(device, q):
         cols = aligned((device * pieces + q) * wide, wide)
@@ -213,8 +251,6 @@
             core_send[dy, q] = product(other + 1 - core, q).astype(jnp.bfloat16)
             core_copy(dy, q).start()
             return 0
-
-        lax.fori_loop(0, pieces, give, 0)
 
         def add(q, _):
             mine = product(other + core, q)
@@ -230,12 +266,23 @@
                 out[:, aligned(q * wide, wide)] = mine.astype(jnp.bfloat16)
             return 0
 
-        lax.fori_loop(0, pieces, add, 0)
+        def both(q, _):
+            give(q + 1, 0)
+            return add(q, 0)
+
+        if dy:
+            give(0, 0)
+            lax.fori_loop(0, pieces - 1, both, 0)
+            add(pieces - 1, 0)
+        else:
+            lax.fori_loop(0, pieces, give, 0)
+            lax.fori_loop(0, pieces, add, 0)
 
     def drain(k, _):
         peer = lax.rem(me + k, lanes)
         values_copy(me, peer).wait_send()
-        mixed_copy(me, peer).wait_send()
+        mixed_copy(me, peer, 0).wait_send()
+        mixed_copy(me, peer, 1).wait_send()
         return 0
 
     lax.fori_loop(1, lanes, drain, 0)
@@ -263,17 +310,23 @@
     wide = own // pieces
     bf16, f32 = jnp.bfloat16, jnp.float32
     vmem = pl.BlockSpec(memory_space=pltpu.VMEM)
+    hbm = pl.BlockSpec(memory_space=pltpu.HBM)
+    taps = short_filter.shape[0]
     dma = pltpu.SemaphoreType.DMA
     return pl.pallas_call(
         functools.partial(fused_kernel, lanes, cores_y),
         out_shape=jax.ShapeDtypeStruct((rows, own), bf16),
-        in_specs=[vmem, vmem, vmem, pl.BlockSpec(memory_space=pl.ANY)],
+        in_specs=[hbm] * 4,
         out_specs=vmem,
         scratch_shapes=[
+            pltpu.VMEM((3, rows, chans), bf16),
+            pltpu.VMEM((3, taps, chans), f32),
+            pltpu.VMEM((groups, reach), bf16),
             pltpu.VMEM((chans, features), bf16),
             pltpu.VMEM((3, EDGE, chans), bf16),
             pltpu.VMEM((groups, reach + 2 * rows), f32),
             pltpu.VMEM((share // GSIZE, reach + rows, rows), bf16),
+            pltpu.VMEM((rows, chans), f32),
             pltpu.VMEM((rows, chans), f32),
             pltpu.VMEM((lanes, share, rows), bf16),
             pltpu.VMEM((behind + lanes, share, rows), bf16),
@@ -284,26 +337,26 @@
             pltpu.VMEM((cores_y, pieces, rows, wide), bf16),
             pltpu.VMEM((cores_y, pieces, rows, wide), bf16),
             pltpu.VMEM((cores_y, pieces, rows, wide), bf16),
-            dma,
+            dma((4,)),
             dma((2,)),
             dma((lanes,)),
             dma((lanes,)),
-            dma((lanes,)),
-            dma((lanes,)),
+            dma((2, lanes)),
+            dma((2, lanes)),
             dma((cores_y, pieces)),
             dma((cores_y, pieces)),
             dma((cores_y, pieces)),
             dma((cores_y, pieces)),
         ],
         compiler_params=pltpu.CompilerParams(
-            collective_id=0, has_side_effects=True, vmem_limit_bytes=48 * 2**20
+            collective_id=0, has_side_effects=True, vmem_limit_bytes=62 * 2**20
         ),
         cost_estimate=pl.CostEstimate(
             flops=2 * rows * chans * features,
             bytes_accessed=2 * chans * features,
             transcendentals=0,
         ),
-    )(jnp.transpose(projected, (1, 0, 2)), short_filter, long_filter, out_weight)
+    )(jnp.transpose(projected, (1, 0, 2)), jnp.transpose(short_filter, (1, 0, 2)), long_filter, out_weight)
 
 
 def fits(projected, long_filter, out_weight):

time: 44.1 us -> 43.8 us (level)
  local copies, waits for them, and re-layouts: 3.72 us -> 1.88 us
  Pallas kernels: 40.1 us -> 41.7 us
    unnamed x6 -> x1, local copies, waits for them, and re-layouts: 3.72 us -> 1.88 us
    pallas_call x1, Pallas kernels: 40.1 us -> 41.7 us  [fused(): pl.pallas_call(functools.partial(fused_kernel, lanes, cores_y), out_shape...]
where the time goes in v2:
time: 43.8 us; the launch traced here: 43.6 us
  Pallas kernels  41.7 us (95%)
  local copies, waits for them, and re-layouts  1.88 us (4%)
    pallas_call x1, Pallas kernels, fused(): pl.pallas_call(functools.partial(fused_kernel, lanes, cores_y), out_shape...  41.7 us
    unnamed x1, local copies, waits for them, and re-layouts  1.88 us

profile of v2, /device:TPU:0, one launch (start us, length us, event | category | flops | bytes accessed | tf_op | source)
XLA Modules:
  0.0 43.6 jit_solution(6648539344855267289)
XLA Ops:
  0.0 41.7 %shard_map.46 = bf16[128,2048]{1,0:T(8,128)(2,1)} custom-call(bf16[3,128,1024]{2,1,0:T(8,128)(2,1)} %bitcast.2, f32[3,7,1024]{2,1,0:T(8,128)} %bitcast.3, bf16[64,512]{1,0:T(8,128)(2,1)} %longf_hbm.1, bf16[1024,8192]{1,0:T(8,128)(2,1)} %weight.1), custom_call_target="tpu_custom_call" | custom-call | flops 2147483648 | bytes 16777216 | tf_op jit(solution)/shard_map/pallas_call | solution.py:316
  41.7 1.9 %copy.6 = bf16[128,2048]{1,0:T(8,128)(2,1)} copy(bf16[128,2048]{1,0:T(8,128)(2,1)} %shard_map.46) | data formatting | bytes 1048576

commit v3 on v2

--- a/solution.py
+++ b/solution.py
@@ -153,6 +153,10 @@
 
     half = share // 2
 
+    def far_first(i):
+        k = lanes // 2 + (i + 1) // 2 * (2 * (i % 2) - 1)
+        return lax.rem(me + k, lanes)
+
     def mixed_copy(slot, peer, h):
         part = pl.ds(h * half, half)
         return pltpu.make_async_remote_copy(
@@ -163,13 +167,13 @@
             device_id={"ctx": peer},
         )
 
-    def send_values(k, _):
-        peer = lax.rem(me + k, lanes)
+    def send_values(i, _):
+        peer = far_first(i)
         send_v[peer] = values_of(peer)
         values_copy(me, peer).start()
         return 0
 
-    lax.fori_loop(1, lanes, send_values, 0)
+    lax.fori_loop(0, lanes - 1, send_values, 0)
     recv_v[behind + me] = values_of(me)
 
     def gates(j, _):
@@ -178,19 +182,19 @@
 
     lax.fori_loop(0, lanes, gates, 0)
 
-    def take_values(k, _):
-        peer = lax.rem(me + k, lanes)
+    def take_values(i, _):
+        peer = far_first(i)
         values_copy(peer, peer).wait_recv()
         return 0
 
-    lax.fori_loop(1, lanes, take_values, 0)
+    lax.fori_loop(0, lanes - 1, take_values, 0)
 
     def send_mixed(h):
-        def start(k, _):
-            mixed_copy(me, lax.rem(me + k, lanes), h).start()
+        def start(i, _):
+            mixed_copy(me, far_first(i), h).start()
             return 0
 
-        lax.fori_loop(1, lanes, start, 0)
+        lax.fori_loop(0, lanes - 1, start, 0)
 
     for g in range(own_groups):
         part = pl.ds(g * GSIZE, GSIZE)
@@ -212,14 +216,14 @@
 
     make_hidden(me)
 
-    def take_mixed(k, _):
-        peer = lax.rem(me + k, lanes)
+    def take_mixed(i, _):
+        peer = far_first(i)
         mixed_copy(peer, peer, 0).wait_recv()
         mixed_copy(peer, peer, 1).wait_recv()
         make_hidden(peer)
         return 0
 
-    lax.fori_loop(1, lanes, take_mixed, 0)
+    lax.fori_loop(0, lanes - 1, take_mixed, 0)
     loads[3].wait()
 
     def product(device, q):
@@ -306,7 +310,7 @@
     share = chans // lanes
     behind = reach // rows
     own = features // devices
-    pieces = 4
+    pieces = 8
     wide = own // pieces
     bf16, f32 = jnp.bfloat16, jnp.float32
     vmem = pl.BlockSpec(memory_space=pltpu.VMEM)
@@ -315,7 +319,7 @@
     dma = pltpu.SemaphoreType.DMA
     return pl.pallas_call(
         functools.partial(fused_kernel, lanes, cores_y),
-        out_shape=jax.ShapeDtypeStruct((rows, own), bf16),
+        out_shape=pltpu.VMEM((rows, own), bf16),
         in_specs=[hbm] * 4,
         out_specs=vmem,
         scratch_shapes=[
@@ -367,10 +371,10 @@
         rows % 128 == 0
         and share % 128 == 0
         and share * lanes == chans
-        and lanes > 1
+        and lanes % 2 == 0
         and devices % 2 == 0
         and long_filter.shape[1] % rows == 0
-        and out_weight.shape[1] % (devices * 512) == 0
+        and out_weight.shape[1] % (devices * 1024) == 0
     )
 
 

time: 43.8 us -> 41.7 us (0.952)
  local copies, waits for them, and re-layouts: 1.88 us -> 0.8 us
  Pallas kernels: 41.7 us -> 40.8 us
    unnamed x1, local copies, waits for them, and re-layouts: 1.88 us -> 0.8 us
    pallas_call x1, Pallas kernels: 41.7 us -> 40.8 us  [fused(): pl.pallas_call(functools.partial(fused_kernel, lanes, cores_y), out_shape...]
where the time goes in v3:
time: 41.7 us; the launch traced here: 41.6 us
  Pallas kernels  40.8 us (98%)
  local copies, waits for them, and re-layouts  0.8 us (2%)
    pallas_call x1, Pallas kernels, fused(): pl.pallas_call(functools.partial(fused_kernel, lanes, cores_y), out_shape...  40.8 us

profile of v3, /device:TPU:0, one launch (start us, length us, event | category | flops | bytes accessed | tf_op | source)
XLA Modules:
  0.0 41.6 jit_solution(5678872303784571370)
XLA Ops:
  0.0 40.8 %shard_map.46 = bf16[128,2048]{1,0:T(8,128)(2,1)S(1)} custom-call(bf16[3,128,1024]{2,1,0:T(8,128)(2,1)} %bitcast.2, f32[3,7,1024]{2,1,0:T(8,128)} %bitcast.3, bf16[64,512]{1,0:T(8,128)(2,1)} %longf_hbm.1, bf16[1024,8192]{1,0:T(8,128)(2,1)} %weight.1), custom_call_target="tpu_custom_call" | custom-call | flops 2147483648 | bytes 16777216 | tf_op jit(solution)/shard_map/pallas_call | solution.py:320
  40.8 0.8 %copy.6 = bf16[128,2048]{1,0:T(8,128)(2,1)} copy(bf16[128,2048]{1,0:T(8,128)(2,1)S(1)} %shard_map.46) | data formatting | bytes 1048576

commit v4 on v3

--- a/solution.py
+++ b/solution.py
@@ -81,23 +81,6 @@
         pl.semaphore_signal(
             barrier, inc=1, device_id={"tp": lax.rem(y + dy, cores_y) * 2 + core}
         )
-    loads[0].wait()
-    groups = longf.shape[0]
-    padded[:, 0:rows] = jnp.zeros((groups, rows), jnp.float32)
-    padded[:, rows : rows + reach] = longf[...].astype(jnp.float32)
-    padded[:, rows + reach :] = jnp.zeros((groups, rows), jnp.float32)
-    recv_v[0:behind] = jnp.zeros((behind, share, rows), jnp.bfloat16)
-
-    def build(g, _):
-        line = padded[pl.ds(me * own_groups + g, 1), :]
-        flat = jnp.broadcast_to(line, (rows, reach + 2 * rows))
-        skewed = pltpu.roll(flat, 0, 1, stride=1, stride_axis=0)
-        for b in range(behind + 1):
-            low = rows + reach - rows * b
-            toeplitz[g, b * rows : (b + 1) * rows, :] = skewed[:, low : low + rows].astype(jnp.bfloat16)
-        return 0
-
-    lax.fori_loop(0, own_groups, build, 0)
     pl.semaphore_wait(barrier, lanes - 1 + 1 + cores_y - 1)
 
     edge = pltpu.make_async_remote_copy(
@@ -108,6 +91,23 @@
         device_id={"ctx": lax.rem(me + 1, lanes)},
     )
     edge.start()
+    loads[0].wait()
+    groups = longf.shape[0]
+    padded[:, 0:rows] = jnp.zeros((groups, rows), jnp.float32)
+    padded[:, rows : rows + reach] = longf[...].astype(jnp.float32)
+    padded[:, rows + reach :] = jnp.zeros((groups, rows), jnp.float32)
+    recv_v[0:behind] = jnp.zeros((behind, share, rows), jnp.bfloat16)
+
+    def build(g, _):
+        line = padded[pl.ds(me * own_groups + g, 1), :]
+        flat = jnp.broadcast_to(line, (rows, reach + 2 * rows))
+        skewed = pltpu.roll(flat, 0, 1, stride=1, stride_axis=0)
+        for b in range(behind + 1):
+            low = rows + reach - rows * b
+            toeplitz[g, b * rows : (b + 1) * rows, :] = skewed[:, low : low + rows].astype(jnp.bfloat16)
+        return 0
+
+    lax.fori_loop(0, own_groups, build, 0)
 
 
     loads[1].wait()
@@ -142,16 +142,17 @@
         values[0:EDGE, cols] = outer(1, j) * outer(2, j)
         return values[:, cols].T.astype(jnp.bfloat16)
 
-    def values_copy(slot, peer):
+    half = share // 2
+
+    def values_copy(slot, peer, h):
+        part = pl.ds(h * half, half)
         return pltpu.make_async_remote_copy(
-            src_ref=send_v.at[peer],
-            dst_ref=recv_v.at[behind + slot],
-            send_sem=v_sems.at[peer],
-            recv_sem=v_recvs.at[slot],
+            src_ref=send_v.at[peer, part],
+            dst_ref=recv_v.at[behind + slot, part],
+            send_sem=v_sems.at[h, peer],
+            recv_sem=v_recvs.at[h, slot],
             device_id={"ctx": peer},
         )
-
-    half = share // 2
 
     def far_first(i):
         k = lanes // 2 + (i + 1) // 2 * (2 * (i % 2) - 1)
@@ -170,10 +171,15 @@
     def send_values(i, _):
         peer = far_first(i)
         send_v[peer] = values_of(peer)
-        values_copy(me, peer).start()
+        values_copy(me, peer, 0).start()
+        return 0
+
+    def send_rest(i, _):
+        values_copy(me, far_first(i), 1).start()
         return 0
 
     lax.fori_loop(0, lanes - 1, send_values, 0)
+    lax.fori_loop(0, lanes - 1, send_rest, 0)
     recv_v[behind + me] = values_of(me)
 
     def gates(j, _):
@@ -182,12 +188,13 @@
 
     lax.fori_loop(0, lanes, gates, 0)
 
-    def take_values(i, _):
-        peer = far_first(i)
-        values_copy(peer, peer).wait_recv()
-        return 0
-
-    lax.fori_loop(0, lanes - 1, take_values, 0)
+    def take_values(h):
+        def take(i, _):
+            peer = far_first(i)
+            values_copy(peer, peer, h).wait_recv()
+            return 0
+
+        lax.fori_loop(0, lanes - 1, take, 0)
 
     def send_mixed(h):
         def start(i, _):
@@ -198,6 +205,8 @@
 
     for g in range(own_groups):
         part = pl.ds(g * GSIZE, GSIZE)
+        if g * GSIZE % half == 0:
+            take_values(g * GSIZE // half)
         lhs = jnp.concatenate(
             [recv_v[b : b + lanes, part, :].reshape(lanes * GSIZE, rows) for b in range(behind + 1)],
             axis=1,
@@ -284,7 +293,8 @@
 
     def drain(k, _):
         peer = lax.rem(me + k, lanes)
-        values_copy(me, peer).wait_send()
+        values_copy(me, peer, 0).wait_send()
+        values_copy(me, peer, 1).wait_send()
         mixed_copy(me, peer, 0).wait_send()
         mixed_copy(me, peer, 1).wait_send()
         return 0
@@ -343,8 +353,8 @@
             pltpu.VMEM((cores_y, pieces, rows, wide), bf16),
             dma((4,)),
             dma((2,)),
-            dma((lanes,)),
-            dma((lanes,)),
+            dma((2, lanes)),
+            dma((2, lanes)),
             dma((2, lanes)),
             dma((2, lanes)),
             dma((cores_y, pieces)),

time: 41.7 us -> 40.7 us (0.976)
  Pallas kernels: 40.8 us -> 39.8 us
    pallas_call x1, Pallas kernels: 40.8 us -> 39.8 us  [fused(): pl.pallas_call(functools.partial(fused_kernel, lanes, cores_y), out_shape...]
where the time goes in v4:
time: 40.7 us; the launch traced here: 40.6 us
  Pallas kernels  39.8 us (98%)
  local copies, waits for them, and re-layouts  0.8 us (2%)
    pallas_call x1, Pallas kernels, fused(): pl.pallas_call(functools.partial(fused_kernel, lanes, cores_y), out_shape...  39.8 us

profile of v4, /device:TPU:0, one launch (start us, length us, event | category | flops | bytes accessed | tf_op | source)
XLA Modules:
  0.0 40.6 jit_solution(17664923976069340429)
XLA Ops:
  0.0 39.8 %shard_map.46 = bf16[128,2048]{1,0:T(8,128)(2,1)S(1)} custom-call(bf16[3,128,1024]{2,1,0:T(8,128)(2,1)} %bitcast.2, f32[3,7,1024]{2,1,0:T(8,128)} %bitcast.3, bf16[64,512]{1,0:T(8,128)(2,1)} %longf_hbm.1, bf16[1024,8192]{1,0:T(8,128)(2,1)} %weight.1), custom_call_target="tpu_custom_call" | custom-call | flops 2147483648 | bytes 16777216 | tf_op jit(solution)/shard_map/pallas_call | solution.py:330
  39.8 0.8 %copy.6 = bf16[128,2048]{1,0:T(8,128)(2,1)} copy(bf16[128,2048]{1,0:T(8,128)(2,1)S(1)} %shard_map.46) | data formatting | bytes 1048576

commit v5 on v4

--- a/solution.py
+++ b/solution.py
@@ -70,7 +70,7 @@
             [(longf_hbm, longf), (proj_hbm, proj), (short_hbm, short), (weight, held_weight)]
         )
     ]
-    for load in loads:
+    for load in loads[:3]:
         load.start()
 
     barrier = pltpu.get_barrier_semaphore()
@@ -107,11 +107,12 @@
             toeplitz[g, b * rows : (b + 1) * rows, :] = skewed[:, low : low + rows].astype(jnp.bfloat16)
         return 0
 
-    lax.fori_loop(0, own_groups, build, 0)
+    lax.fori_loop(0, own_groups, build, 0, unroll=2)
 
 
     loads[1].wait()
     loads[2].wait()
+    loads[3].start()
 
     def taps_over(ext, p, cols):
         total = short[p, 0:1, cols] * ext[EDGE:]
@@ -134,7 +135,7 @@
         gate[EDGE:, cols] = inner(0, j)
         return 0
 
-    lax.fori_loop(0, lanes, inner_rows, 0)
+    lax.fori_loop(0, lanes, inner_rows, 0, unroll=2)
     edge.wait()
 
     def values_of(j):

time: 40.7 us -> 40.7 us (level)
  no operation moved by 1% of the time
where the time goes in v5:
time: 40.7 us; the launch traced here: 40.6 us
  Pallas kernels  39.8 us (98%)
  local copies, waits for them, and re-layouts  0.8 us (2%)
    pallas_call x1, Pallas kernels, fused(): pl.pallas_call(functools.partial(fused_kernel, lanes, cores_y), out_shape...  39.8 us

profile of v5, /device:TPU:0, one launch (start us, length us, event | category | flops | bytes accessed | tf_op | source)
XLA Modules:
  0.0 40.6 jit_solution(14735914784581893940)
XLA Ops:
  0.0 39.8 %shard_map.46 = bf16[128,2048]{1,0:T(8,128)(2,1)S(1)} custom-call(bf16[3,128,1024]{2,1,0:T(8,128)(2,1)} %bitcast.2, f32[3,7,1024]{2,1,0:T(8,128)} %bitcast.3, bf16[64,512]{1,0:T(8,128)(2,1)} %longf_hbm.1, bf16[1024,8192]{1,0:T(8,128)(2,1)} %weight.1), custom_call_target="tpu_custom_call" | custom-call | flops 2147483648 | bytes 16777216 | tf_op jit(solution)/shard_map/pallas_call | solution.py:331
  39.8 0.8 %copy.6 = bf16[128,2048]{1,0:T(8,128)(2,1)} copy(bf16[128,2048]{1,0:T(8,128)(2,1)S(1)} %shard_map.46) | data formatting | bytes 1048576

commit v6 on v5

--- a/solution.py
+++ b/solution.py
@@ -179,7 +179,7 @@
         values_copy(me, far_first(i), 1).start()
         return 0
 
-    lax.fori_loop(0, lanes - 1, send_values, 0)
+    lax.fori_loop(0, lanes - 1, send_values, 0, unroll=True)
     lax.fori_loop(0, lanes - 1, send_rest, 0)
     recv_v[behind + me] = values_of(me)
 
@@ -187,7 +187,7 @@
         gate[0:EDGE, aligned(j * share, share)] = outer(0, j)
         return 0
 
-    lax.fori_loop(0, lanes, gates, 0)
+    lax.fori_loop(0, lanes, gates, 0, unroll=2)
 
     def take_values(h):
         def take(i, _):

time: 40.7 us -> 40.7 us (level)
  no operation moved by 1% of the time
where the time goes in v6:
time: 40.7 us; the launch traced here: 40.6 us
  Pallas kernels  39.8 us (98%)
  local copies, waits for them, and re-layouts  0.8 us (2%)
    pallas_call x1, Pallas kernels, fused(): pl.pallas_call(functools.partial(fused_kernel, lanes, cores_y), out_shape...  39.8 us

profile of v6, /device:TPU:0, one launch (start us, length us, event | category | flops | bytes accessed | tf_op | source)
XLA Modules:
  0.0 40.6 jit_solution(2220145365892260950)
XLA Ops:
  0.0 39.8 %shard_map.46 = bf16[128,2048]{1,0:T(8,128)(2,1)S(1)} custom-call(bf16[3,128,1024]{2,1,0:T(8,128)(2,1)} %bitcast.2, f32[3,7,1024]{2,1,0:T(8,128)} %bitcast.3, bf16[64,512]{1,0:T(8,128)(2,1)} %longf_hbm.1, bf16[1024,8192]{1,0:T(8,128)(2,1)} %weight.1), custom_call_target="tpu_custom_call" | custom-call | flops 2147483648 | bytes 16777216 | tf_op jit(solution)/shard_map/pallas_call | solution.py:331
  39.8 0.8 %copy.6 = bf16[128,2048]{1,0:T(8,128)(2,1)} copy(bf16[128,2048]{1,0:T(8,128)(2,1)S(1)} %shard_map.46) | data formatting | bytes 1048576
